TPU v7x, 256 devices: a whole 4x4x8 slice. The times are simulated.
256 devices in a mesh: sector: 32 (over x, z), term: 8 (over y, core).
Axes of the slice: x: 4, y: 4, z: 8, core: 2. Of those that a mesh axis runs over, the one named last changes fastest.
Arguments:
- wavefunction: bfloat16 [256, 256, 256], P('sector', 'term'), may hold values from -6 to 6
- left_ops: bfloat16 [64, 256, 256, 256], P('term', 'sector'), may hold values from -0.375 to 0.375
- right_ops: bfloat16 [64, 256, 256], P('term'), may hold values from -0.046875 to 0.046875
- term_type: int32 [64], P('term'), may hold values from 0 to 1
- target_slots: int32 [2, 256], replicated, may hold values from 0 to 255, as said below
- block_rows: int32 [256], replicated, may hold values from 1 to 256, 32768 in all
Outputs:
- sigma_blocks: bfloat16 [256, 256, 256], P('sector', 'term')
Inputs may be any that keep to these rules, and one draw needn't show every extreme that they name: Each row target_slots[g] is a permutation of the 256 slots. Slots i * 8 to (i + 1) * 8 - 1 lie on device i of the sector axis, and the 16 entries of one device's slots (both rows together) name slots of any one device at most 1 times; that most is reached. `block_rows`: some block uses all 256 rows.
All inputs are finite; a program needn't handle non-finite values.
Results may differ from a plain program's by a relative error of at most 0.0049.
Values may be sent and summed in bfloat16 or wider, within the bound.
A program may use at most 128 MiB of HBM per device.

v0:
```python
import jax
import jax.numpy as jnp
from jax import lax
from jax.sharding import PartitionSpec as P

TYPES = 2


def routing(target_slots, sec_count, group_count, my_index):
    item_count = TYPES * sec_count
    peer_cap = max(1, item_count // group_count)
    slot_table = (
        target_slots.reshape(TYPES, group_count, sec_count)
        .transpose(1, 0, 2)
        .reshape(group_count, item_count)
    )
    my_slots = lax.dynamic_index_in_dim(slot_table, my_index, 0, keepdims=False)
    my_peer = my_slots // sec_count
    peer_ids = jnp.arange(group_count, dtype=jnp.int32)
    matches = (my_peer[:, None] == peer_ids[None, :]).astype(jnp.int32)
    my_rank = jnp.sum((jnp.cumsum(matches, axis=0) - 1) * matches, axis=1)
    send_pos = my_peer * peer_cap + my_rank
    fill_src = (
        jnp.full((group_count * peer_cap,), item_count, jnp.int32)
        .at[send_pos]
        .set(jnp.arange(item_count, dtype=jnp.int32), mode="drop")
    )
    arriving = slot_table // sec_count == my_index
    arrival_rank = jnp.cumsum(arriving.astype(jnp.int32), axis=1) - 1
    position = peer_ids[:, None] * peer_cap + arrival_rank
    type_index = jnp.arange(item_count, dtype=jnp.int32) // sec_count
    target_index = jnp.where(
        arriving, slot_table % sec_count * TYPES + type_index[None, :], item_count
    )
    source_pos = (
        jnp.zeros((item_count,), jnp.int32)
        .at[target_index.reshape(-1)]
        .set(position.reshape(-1), mode="drop")
    )
    return (fill_src, source_pos)


def pack_outgoing(flattened, fill_src):
    item_count = flattened.shape[0]
    valid = fill_src < item_count
    picked = flattened[jnp.minimum(fill_src, item_count - 1)]
    return jnp.where(valid[:, None, None], picked, jnp.zeros((), picked.dtype))


def combine(received, source_pos, sec_count):
    selected = received[source_pos]
    selected = selected.reshape((sec_count, TYPES) + received.shape[1:])
    return jnp.sum(selected, axis=1)


def local(wavefunction, left_ops, right_ops, term_type, target_slots, block_rows):
    sec_count = wavefunction.shape[0]
    group_count = lax.axis_size("sector")
    my_index = lax.axis_index("sector")
    gathered = lax.all_gather(wavefunction, "term", axis=1, tiled=True)
    full_rows = gathered.shape[1]
    own_rows = lax.dynamic_slice_in_dim(block_rows, my_index * sec_count, sec_count)
    row_mask = jnp.arange(full_rows, dtype=jnp.int32)[None, :] < own_rows[:, None]
    masked = jnp.where(row_mask[:, :, None], gathered, jnp.zeros((), gathered.dtype))
    totals = jnp.zeros((TYPES,) + masked.shape, jnp.float32)
    for term_step in range(left_ops.shape[0]):
        half_step = jnp.einsum(
            "sab,sbc->sac", left_ops[term_step], masked, preferred_element_type=jnp.float32
        ).astype(jnp.bfloat16)
        term_block = jnp.einsum(
            "sac,cd->sad", half_step, right_ops[term_step], preferred_element_type=jnp.float32
        )
        op_type = term_type[term_step]
        updated = lax.dynamic_index_in_dim(totals, op_type, 0, keepdims=False) + term_block
        totals = lax.dynamic_update_index_in_dim(totals, updated, op_type, 0)
    fill_src, source_pos = routing(target_slots, sec_count, group_count, my_index)
    outgoing = pack_outgoing(totals.reshape((TYPES * sec_count,) + masked.shape[1:]), fill_src)
    received = lax.all_to_all(outgoing, "sector", split_axis=0, concat_axis=0, tiled=True)
    partial_value = combine(received, source_pos, sec_count)
    partial_value = jnp.where(
        row_mask[:, :, None], partial_value, jnp.zeros((), partial_value.dtype)
    )
    result = lax.psum_scatter(partial_value, "term", scatter_dimension=1, tiled=True)
    return result.astype(jnp.bfloat16)


def solution(mesh):
    in_specs = (
        P("sector", "term", None),
        P("term", "sector", None, None),
        P("term", None, None),
        P("term"),
        P(),
        P(),
    )
    out_specs = P("sector", "term", None)
    return jax.shard_map(local, mesh=mesh, in_specs=in_specs, out_specs=out_specs, check_vma=False)
```

profile of v0, /device:TPU:1, one launch (start us, length us, event | category | flops | bytes accessed | tf_op | source)
XLA Modules:
  0.0 359.9 jit_solution(5389014352389649103)
XLA Ops:
  6.5 0.7 all-gather.2.cloned.1.call-update
  7.3 1.6 fusion.84
  18.8 0.8 reshape.276
  19.9 0.8 dynamic_slice.30
  25.9 0.6 scatter_custom_fusion
  26.6 12.8 %all-gather.2.cloned.1.call-done = bf16[8,256,256]{2,1,0:T(8,128)(2,1)} async-done(((bf16[8,32,256]{2,1,0:T(8,128)(2,1)}), bf16[8,256,256]{2,1,0:T(8,128)(2,1)}) %all-gather.2.cloned.1.call-update) | async-done | bytes 1048592 | tf_op jit(solution)/shard_map/all_gather | solution.py:60
  39.4 2.4 broadcast_in_dim.85
  41.8 3.6 %bitcast_dynamic-update-slice_fusion.7 = f32[2,8,256,256]{3,2,1,0:T(8,128)} fusion(f32[2,8,256,256]{3,2,1,0:T(8,128)} %broadcast_in_dim.85, s32[]{:T(128)S(6)} %select_n.151, bf16[8,8,256,256]{3,2,1,0:T(8,128)(2,1)} %param.7, bf16[8,256,256]{2,1,0:T(8,128)(2,1)S(1)} %copy-done, pred[8,256]{1,0:T(8,128)(4,1)S(1)} %iota_compare_fusion.1, ...), kind=kOutput, calls=%fused_computation.20 | convolution fusion | flops 537919488 | bytes 4327428 | tf_op jit(solution)/shard_map/sac,cd->sad/dot_general | solution.py:70
  45.4 1.8 constant_dynamic-slice_fusion.6
  47.2 3.6 bitcast_dynamic-update-slice_fusion.6
  50.8 1.8 constant_dynamic-slice_fusion.5
  52.7 3.6 %bitcast_dynamic-update-slice_fusion.5 = f32[2,8,256,256]{3,2,1,0:T(8,128)} fusion(f32[2,8,256,256]{3,2,1,0:T(8,128)} %bitcast_dynamic-update-slice_fusion.6, s32[]{:T(128)S(6)} %select_n.153, f32[1,8,256,256]{3,2,1,0:T(8,128)S(1)} %constant_dynamic-slice_fusion.5, bf16[8,8,256,256]{3,2,1,0:T(8,128)(2,1)} %param.7, bf16[8,256,256]{2,1,0:T(8,128)(2,1)S(1)} %copy-done, ...), kind=kOutput, calls=%fused_computation.16 | convolution fusion | flops 538443776 | bytes 6424580 | tf_op jit(solution)/shard_map/sac,cd->sad/dot_general | solution.py:70
  56.3 1.8 constant_dynamic-slice_fusion.4
  58.1 3.6 %bitcast_dynamic-update-slice_fusion.4 = f32[2,8,256,256]{3,2,1,0:T(8,128)} fusion(f32[2,8,256,256]{3,2,1,0:T(8,128)} %bitcast_dynamic-update-slice_fusion.5, s32[]{:T(128)S(6)} %select_n.154, f32[1,8,256,256]{3,2,1,0:T(8,128)S(1)} %constant_dynamic-slice_fusion.4, bf16[8,8,256,256]{3,2,1,0:T(8,128)(2,1)} %param.7, bf16[8,256,256]{2,1,0:T(8,128)(2,1)S(1)} %copy-done, ...), kind=kOutput, calls=%fused_computation.14 | convolution fusion | flops 538443776 | bytes 6424580 | tf_op jit(solution)/shard_map/sac,cd->sad/dot_general | solution.py:70
  61.7 1.8 constant_dynamic-slice_fusion.3
  63.5 3.7 %bitcast_dynamic-update-slice_fusion.3 = f32[2,8,256,256]{3,2,1,0:T(8,128)} fusion(f32[2,8,256,256]{3,2,1,0:T(8,128)} %bitcast_dynamic-update-slice_fusion.4, s32[]{:T(128)S(6)} %select_n.155, f32[1,8,256,256]{3,2,1,0:T(8,128)S(1)} %constant_dynamic-slice_fusion.3, bf16[8,8,256,256]{3,2,1,0:T(8,128)(2,1)} %param.7, bf16[8,256,256]{2,1,0:T(8,128)(2,1)S(1)} %copy-done, ...), kind=kOutput, calls=%fused_computation.12 | convolution fusion | flops 538443776 | bytes 6424580 | tf_op jit(solution)/shard_map/sac,cd->sad/dot_general | solution.py:70
  67.1 1.8 constant_dynamic-slice_fusion.2
  69.0 3.6 %bitcast_dynamic-update-slice_fusion.2 = f32[2,8,256,256]{3,2,1,0:T(8,128)} fusion(f32[2,8,256,256]{3,2,1,0:T(8,128)} %bitcast_dynamic-update-slice_fusion.3, s32[]{:T(128)S(6)} %select_n.156, f32[1,8,256,256]{3,2,1,0:T(8,128)S(1)} %constant_dynamic-slice_fusion.2, bf16[8,8,256,256]{3,2,1,0:T(8,128)(2,1)} %param.7, bf16[8,256,256]{2,1,0:T(8,128)(2,1)S(1)} %copy-done, ...), kind=kOutput, calls=%fused_computation.10 | convolution fusion | flops 538443776 | bytes 6424580 | tf_op jit(solution)/shard_map/sac,cd->sad/dot_general | solution.py:70
  72.6 1.8 constant_dynamic-slice_fusion.1
  74.4 3.7 %bitcast_dynamic-update-slice_fusion.1 = f32[2,8,256,256]{3,2,1,0:T(8,128)} fusion(f32[2,8,256,256]{3,2,1,0:T(8,128)} %bitcast_dynamic-update-slice_fusion.2, s32[]{:T(128)S(6)} %select_n.157, f32[1,8,256,256]{3,2,1,0:T(8,128)S(1)} %constant_dynamic-slice_fusion.1, bf16[8,8,256,256]{3,2,1,0:T(8,128)(2,1)} %param.7, bf16[8,256,256]{2,1,0:T(8,128)(2,1)S(1)} %copy-done, ...), kind=kOutput, calls=%fused_computation.8 | convolution fusion | flops 538443776 | bytes 6424580 | tf_op jit(solution)/shard_map/sac,cd->sad/dot_general | solution.py:70
  78.0 1.8 constant_dynamic-slice_fusion
  79.9 3.7 %bitcast_dynamic-update-slice_fusion = f32[2,8,256,256]{3,2,1,0:T(8,128)} fusion(f32[2,8,256,256]{3,2,1,0:T(8,128)} %bitcast_dynamic-update-slice_fusion.1, s32[]{:T(128)S(6)} %select_n.158, f32[1,8,256,256]{3,2,1,0:T(8,128)S(1)} %constant_dynamic-slice_fusion, bf16[8,8,256,256]{3,2,1,0:T(8,128)(2,1)} %param.7, bf16[8,256,256]{2,1,0:T(8,128)(2,1)S(1)} %copy-done, ...), kind=kOutput, calls=%fused_computation.6 | convolution fusion | flops 538443776 | bytes 6424580 | tf_op jit(solution)/shard_map/sac,cd->sad/dot_general | solution.py:70
  83.5 6.5 %gather_fusion = f32[32,256,256]{2,1,0:T(8,128)} fusion(f32[16,256,256]{2,1,0:T(8,128)} %bitcast.172, s32[1024]{0:T(1024)S(1)} %pad_clamp_fusion.1), kind=kCustom, calls=%fused_computation | custom fusion | bytes 16777344 | tf_op jit(solution)/shard_map/gather | solution.py:46
  90.0 7.8 %broadcast_select_fusion = f32[32,256,256]{2,1,0:T(8,128)} fusion(f32[32,256,256]{2,1,0:T(8,128)} %gather_fusion, pred[32]{0:T(512)(128)(4,1)S(1)} %broadcast_compare_fusion), kind=kLoop, calls=%fused_computation.5 | loop fusion | flops 2097152 | bytes 16777248 | tf_op jit(solution)/shard_map/jit(_where)/select_n | solution.py:47
  97.8 9.7 %all-to-all-start = ((f32[32,256,256]{2,1,0:T(8,128)}), f32[32,256,256]{2,1,0:T(8,128)}, u32[]{:S(2)}, u32[]{:S(2)}) async-start(f32[32,256,256]{2,1,0:T(8,128)} %broadcast_select_fusion), calls=%async_computation | async-start | bytes 16777216 | tf_op jit(solution)/shard_map/all_to_all | solution.py:78
  108.2 2.4 scatter_custom_fusion.1
  110.6 186.0 %all-to-all-done = f32[32,256,256]{2,1,0:T(8,128)} async-done(((f32[32,256,256]{2,1,0:T(8,128)}), f32[32,256,256]{2,1,0:T(8,128)}, u32[]{:S(2)}, u32[]{:S(2)}) %all-to-all-start) | async-done | bytes 8388640 | tf_op jit(solution)/shard_map/all_to_all | solution.py:78
  296.6 6.2 %gather_fusion.1 = f32[16,256,256]{2,1,0:T(8,128)} fusion(f32[32,256,256]{2,1,0:T(8,128)} %all-to-all-done, s32[1024]{0:T(1024)S(1)} %pad_clamp_fusion), kind=kCustom, calls=%fused_computation.1 | custom fusion | bytes 8388672 | tf_op jit(solution)/shard_map/gather | solution.py:51
  302.8 2.7 bitcast_reduce_fusion
  305.5 1.7 broadcast_select_fusion.1
  307.2 44.2 %reduce-scatter.2.cloned.1.call-done = f32[8,32,256]{2,1,0:T(8,128)} async-done(((f32[8,256,256]{2,1,0:T(8,128)}), f32[8,32,256]{2,1,0:T(8,128)}) %reduce-scatter.2.cloned.1.call-update) | async-done | bytes 262160 | tf_op jit(solution)/shard_map/reduce_scatter | solution.py:83
  351.4 1.6 convert_element_type.75
  (29 shorter events, 1.3 us)
Async XLA Ops:
  6.5 32.9 %all-gather.2.cloned.1.call-start = ((), (), s32[]{:S(2)}) async-start(), calls=%async_computation.2 | async-start | bytes 1179648 | tf_op jit(solution)/shard_map/all_gather | solution.py:60
  39.4 2.4 copy-start
  97.8 198.8 %all-to-all-start = ((f32[32,256,256]{2,1,0:T(8,128)}), f32[32,256,256]{2,1,0:T(8,128)}, u32[]{:S(2)}, u32[]{:S(2)}) async-start(f32[32,256,256]{2,1,0:T(8,128)} %broadcast_select_fusion), calls=%async_computation | async-start | bytes 16777216 | tf_op jit(solution)/shard_map/all_to_all | solution.py:78
  107.5 244.0 %reduce-scatter.2.cloned.1.call-start = ((), (), s32[]{:S(2)}) async-start(), calls=%async_computation.3 | async-start | bytes 2359296 | tf_op jit(solution)/shard_map/reduce_scatter | solution.py:83
Sparse Core Ops, SparseCore 0:
  9.2 30.1 all-gather.1
  307.4 44.0 reduce-scatter.1
where the time goes:
time: 363 us; the launch traced here: 360 us
  waiting for transfers between devices  244 us (67%)
  local copies, waits for them, and re-layouts  34.5 us (10%)
  matrix products  29 us (8%)
  between operations  28.4 us (8%)
  other arithmetic  14.5 us (4%)
  starting transfers between devices  9.71 us (3%)
    all_to_all x1, waiting for transfers between devices, local(): lax.all_to_all(outgoing, 'sector', split_axis=0, concat_axis=0, tiled=True)  186 us
    reduce_scatter x1, waiting for transfers between devices, local(): lax.psum_scatter(partial_value, 'term', scatter_dimension=1, tiled=True)  44.2 us
    dot_general x8, matrix products, local(): jnp.einsum('sac,cd->sad', half_step, right_ops[term_step], preferred_elem...  29 us
    all_gather x1, waiting for transfers between devices, local(): gathered = lax.all_gather(wavefunction, 'term', axis=1, tiled=True)  12.8 us
    dynamic_slice x7, local copies, waits for them, and re-layouts, local(): lax.dynamic_index_in_dim(totals, op_type, 0, keepdims=False) + term_block  12.7 us
    all_to_all x1, starting transfers between devices, local(): lax.all_to_all(outgoing, 'sector', split_axis=0, concat_axis=0, tiled=True)  9.66 us
    select_n x1, other arithmetic, pack_outgoing(): return jnp.where(valid[:, None, None], picked, jnp.zeros((), picked.dtype))  7.81 us
  transfers between devices with their start and end apart: 3, of which 3 were waited for; matrix products, arithmetic and copies ran while one was open for 2% of the time, Pallas kernels for 0%

commit v1 on v0

v1 whole, which is shorter than its diff:
```python
import jax
import jax.numpy as jnp
from jax import lax
from jax.experimental import pallas as pl
from jax.experimental.pallas import tpu as pltpu
from jax.sharding import PartitionSpec as P

MESH = pl.DeviceIdType.MESH
BF, F32 = jnp.bfloat16, jnp.float32
N = 256
S = 8
K = 8
G = 2
Y = 4
J = 8
D = 32
H = 2
R = N // J // H
C = 2
SC = S // C


def kernel(
    wf, left, right, types, slots, rows,
    out,
    left_v, right_v, rcat, gath, masked, half, own, d2d_out, d2d_in, y_out, y_in,
    items, a2a_out, a2a_in, tab_v, tab,
    left_sem, misc_sem, ag_send, ag_recv, d2d_send, d2d_recv, y_send, y_recv, a2a_send, a2a_recv,
):
    me_s, me_t = lax.axis_index("sector"), lax.axis_index("term")
    y, c = me_t // 2, me_t % 2
    sib = y * 2 + (1 - c)

    def term_copy(src, dst, send, recv, to):
        return pltpu.make_async_remote_copy(
            src_ref=src, dst_ref=dst, send_sem=send, recv_sem=recv,
            device_id={"term": to}, device_id_type=MESH,
        )

    def y_peer(d):
        return lax.rem(y + d, Y) * 2 + c

    right_copy = pltpu.make_async_copy(right, right_v, misc_sem.at[0])
    right_copy.start()
    left_copies = {}
    for h in range(H):
        for o in range(2):
            side = 1 - c if o == 0 else c
            for s in range(S):
                cp = pltpu.make_async_copy(
                    left.at[:, s, :, side, h], left_v.at[h, o, s], left_sem.at[h, o, s]
                )
                cp.start()
                left_copies[h, o, s] = cp
    own_copy = pltpu.make_async_copy(wf, gath.at[:, me_t], misc_sem.at[1])
    own_copy.start()

    barrier = pltpu.get_barrier_semaphore()
    pl.semaphore_signal(barrier, inc=1, device_id={"term": sib}, device_id_type=MESH)
    for d in range(1, Y):
        pl.semaphore_signal(barrier, inc=1, device_id={"term": y_peer(d)}, device_id_type=MESH)

    @pl.loop(1, D)
    def _(q):
        pl.semaphore_signal(
            barrier, inc=1, device_id={"sector": lax.rem(me_s + q, D)}, device_id_type=MESH
        )

    pl.semaphore_wait(barrier, 1 + (Y - 1) + (D - 1))

    pending = []
    first = {}
    for p in range(C):
        part = pl.ds(p * SC, SC)
        for d in (1, 3, 2):
            cp = term_copy(
                wf.at[part], gath.at[part, me_t], ag_send.at[p, d], ag_recv.at[p, d], y_peer(d)
            )
            cp.start()
            first[p, d] = cp
        cp = term_copy(wf.at[part], gath.at[part, me_t], ag_send.at[p, 0], ag_recv.at[p, 0], sib)
        cp.start()
        first[p, 0] = cp

    lane = lax.broadcasted_iota(jnp.int32, (D, D * S), 1)
    peer = lax.broadcasted_iota(jnp.int32, (D, D * S), 0)
    mine = lax.shift_right_logical(lane, 3) == me_s
    item = jnp.zeros((D, D * S), jnp.int32)
    target = lax.broadcasted_iota(jnp.int32, (S, D * S), 0) + me_s * S
    lane_s = lax.broadcasted_iota(jnp.int32, (S, D * S), 1)
    for g in range(G):
        row = slots[g : g + 1, :]
        hit = mine & (lax.shift_right_logical(row, 3) == peer)
        item = jnp.maximum(item, jnp.where(hit, jnp.bitwise_and(lane, 7) + g * S, 0))
        src = jnp.where(row == target, lax.shift_right_logical(lane_s, 3), 0)
        tab_v[D + g * S : D + (g + 1) * S, :] = jnp.broadcast_to(
            jnp.max(src, axis=1, keepdims=True), (S, 128)
        )
    tab_v[0:D, :] = jnp.broadcast_to(jnp.max(item, axis=1, keepdims=True), (D, 128))
    tab_copy = pltpu.make_async_copy(tab_v, tab, misc_sem.at[2])
    tab_copy.start()

    right_copy.wait()
    for k in range(K):
        for g in range(G):
            rcat[k * N : (k + 1) * N, g * N : (g + 1) * N] = jnp.where(
                types[k] == g, right_v[k].astype(F32), 0.0
            ).astype(BF)

    own_copy.wait()
    for p in range(C):
        part = pl.ds(p * SC, SC)
        for d in (1, 3, 2):
            first[p, d].wait_recv()
            owner = lax.rem(y + Y - d, Y) * 2 + c
            block = gath.at[part, owner]
            cp = term_copy(block, block, ag_send.at[p, 3 + d], ag_recv.at[p, 3 + d], sib)
            cp.start()
            first[p, 3 + d] = cp
        first[p, 0].wait_recv()
        for d in (1, 3, 2):
            first[p, 3 + d].wait_recv()
        for s in range(p * SC, (p + 1) * SC):
            row_id = lax.broadcasted_iota(jnp.int32, (N, N), 0)
            block = gath[s].reshape(N, N).astype(F32)
            masked[s] = jnp.where(row_id < rows[me_s * S + s], block, 0.0).astype(BF)
    pending += list(first.values())

    def unit(h, o):
        for s in range(S):
            left_copies[h, o, s].wait()

        @pl.loop(0, S)
        def _(s):
            lhs = left_v[h, o, s].reshape(K * Y * R, N)
            res = jnp.dot(lhs, masked[s], preferred_element_type=F32).astype(BF)
            for k in range(K):
                half[s, :, k * N : (k + 1) * N] = res[k * Y * R : (k + 1) * Y * R]

        def second(s):
            lhs = half[pl.ds(s * 4, 4)].reshape(4 * Y * R, K * N)
            return jnp.dot(lhs, rcat[...], preferred_element_type=F32).reshape(4, Y, R, G * N)

        @pl.loop(0, S // 4)
        def _(s):
            if o == 0:
                d2d_out[h, pl.ds(s * 4, 4)] = second(s).astype(BF)
            else:
                own[h, pl.ds(s * 4, 4)] = second(s)

    def send_d2d(h):
        cp = term_copy(d2d_out.at[h], d2d_in.at[h], d2d_send.at[h], d2d_recv.at[h], sib)
        cp.start()
        pending.append(cp)
        return cp

    def send_y(h, d2d):
        d2d.wait_recv()
        copies = []
        for d in (2, 1, 3):
            to = lax.rem(y + d, Y)
            y_out[h, d - 1] = (own[h, :, to] + d2d_in[h, :, to].astype(F32)).astype(BF)
            cp = term_copy(
                y_out.at[h, d - 1], y_in.at[h, d - 1], y_send.at[h, d - 1], y_recv.at[h, d - 1], y_peer(d)
            )
            cp.start()
            copies.append(cp)
        pending.extend(copies)
        return copies

    def send_a2a(h, copies):
        for cp in copies:
            cp.wait_recv()
        total = own[h, :, y] + d2d_in[h, :, y].astype(F32)
        for d in range(1, Y):
            total = total + y_in[h, d - 1].astype(F32)
        total = total.astype(BF)
        for g in range(G):
            items[h, g * S : (g + 1) * S] = total[:, :, g * N : (g + 1) * N]

        @pl.loop(0, D)
        def _(p):
            a2a_out[h, p] = items[h, tab[p, 0]]

        a2a_in[h][me_s] = items[h, tab[me_s, 0]]

        @pl.loop(1, D)
        def _(q):
            p = lax.rem(me_s + q, D)
            pltpu.make_async_remote_copy(
                src_ref=a2a_out.at[h, p], dst_ref=a2a_in[h].at[me_s],
                send_sem=a2a_send.at[h], recv_sem=a2a_recv.at[h],
                device_id={"sector": p}, device_id_type=MESH,
            ).start()

    def combine(h):
        got = a2a_in[h].at[pl.ds(0, D - 1)]
        pltpu.make_async_copy(got, got, a2a_recv.at[h]).wait()
        first_row = me_t * (H * R) + h * R
        for t in range(S):
            value = a2a_in[h][tab[D + t, 0]].astype(F32) + a2a_in[h][tab[D + S + t, 0]].astype(F32)
            row_id = lax.broadcasted_iota(jnp.int32, (R, N), 0) + first_row
            value = jnp.where(row_id < rows[me_s * S + t], value, 0.0)
            out[t, h * R : (h + 1) * R] = value.astype(BF)

    unit(0, 0)
    d2d0 = send_d2d(0)
    unit(0, 1)
    y0 = send_y(0, d2d0)
    unit(1, 0)
    d2d1 = send_d2d(1)
    unit(1, 1)
    y1 = send_y(1, d2d1)
    tab_copy.wait()
    send_a2a(0, y0)
    send_a2a(1, y1)
    combine(0)
    combine(1)
    for cp in pending:
        cp.wait_send()
    for h in range(H):
        sent = a2a_out.at[h, pl.ds(0, D - 1)]
        pltpu.make_async_copy(sent, sent, a2a_send.at[h]).wait()


def local(wavefunction, left_ops, right_ops, term_type, target_slots, block_rows):
    left = left_ops.reshape(K, S, Y, 2, H, R, N)
    any_space = pl.BlockSpec(memory_space=pl.ANY)
    smem = pl.BlockSpec(memory_space=pltpu.SMEM)
    vmem = pl.BlockSpec(memory_space=pltpu.VMEM)
    dma = pltpu.SemaphoreType.DMA
    return pl.pallas_call(
        kernel,
        out_shape=jax.ShapeDtypeStruct((S, N // J, N), BF),
        in_specs=[any_space, any_space, any_space, smem, vmem, smem],
        out_specs=vmem,
        scratch_shapes=[
            pltpu.VMEM((H, 2, S, K, Y, R, N), BF),
            pltpu.VMEM((K, N, N), BF),
            pltpu.VMEM((K * N, G * N), BF),
            pltpu.VMEM((S, J, N // J, N), BF),
            pltpu.VMEM((S, N, N), BF),
            pltpu.VMEM((S, Y * R, K * N), BF),
            pltpu.VMEM((H, S, Y, R, G * N), F32),
            pltpu.VMEM((H, S, Y, R, G * N), BF),
            pltpu.VMEM((H, S, Y, R, G * N), BF),
            pltpu.VMEM((H, Y - 1, S, R, G * N), BF),
            pltpu.VMEM((H, Y - 1, S, R, G * N), BF),
            pltpu.VMEM((H, G * S, R, N), BF),
            pltpu.VMEM((H, D, R, N), BF),
            [pltpu.VMEM((D, R, N), BF)] * H,
            pltpu.VMEM((D + G * S, 128), jnp.int32),
            pltpu.SMEM((D + G * S, 128), jnp.int32),
            dma((H, 2, S)),
            dma((3,)),
            dma((C, 7)),
            dma((C, 7)),
            dma((H,)),
            dma((H,)),
            dma((H, Y - 1)),
            dma((H, Y - 1)),
            dma((H,)),
            dma((H,)),
        ],
        compiler_params=pltpu.CompilerParams(
            collective_id=0, has_side_effects=True, vmem_limit_bytes=56 * 1024 * 1024
        ),
    )(wavefunction, left, right_ops, term_type, target_slots, block_rows)


def solution(mesh):
    in_specs = (
        P("sector", "term", None),
        P("term", "sector", None, None),
        P("term", None, None),
        P("term"),
        P(),
        P(),
    )
    out_specs = P("sector", "term", None)
    return jax.shard_map(local, mesh=mesh, in_specs=in_specs, out_specs=out_specs, check_vma=False)
```

time: 363 us -> 53.8 us (0.15)
  waiting for transfers between devices: 244 us -> 0 us
  Pallas kernels: 0 us -> 52.1 us
  local copies, waits for them, and re-layouts: 34.5 us -> 1.57 us
  matrix products: 29 us -> 0 us
  between operations: 28.4 us -> 0.01 us
  other arithmetic: 14.5 us -> 0 us
  starting transfers between devices: 9.71 us -> 0 us
    all_to_all x1 -> x0, waiting for transfers between devices: 186 us -> none  [local(): lax.all_to_all(outgoing, 'sector', split_axis=0, concat_axis=0, tiled=True)]
    pallas_call x0 -> x1, Pallas kernels: none -> 52.1 us  [local(): pl.pallas_call(kernel, out_shape=jax.ShapeDtypeStruct((S, N // J, N), BF)...]
    reduce_scatter x1 -> x0, waiting for transfers between devices: 44.2 us -> none  [local(): lax.psum_scatter(partial_value, 'term', scatter_dimension=1, tiled=True)]
    dot_general x8 -> x0, matrix products: 29 us -> none  [local(): jnp.einsum('sac,cd->sad', half_step, right_ops[term_step], preferred_elem...]
    dynamic_slice x9 -> x0, local copies, waits for them, and re-layouts: 13.6 us -> none  [the longest x7 12.7 us: local(): lax.dynamic_index_in_dim(totals, op_type, 0, keepdims=False) + term_block]
    all_gather x1 -> x0, waiting for transfers between devices: 12.8 us -> none  [local(): gathered = lax.all_gather(wavefunction, 'term', axis=1, tiled=True)]
    gather x2 -> x0, local copies, waits for them, and re-layouts: 12.6 us -> none  [the longest x1 6.48 us: pack_outgoing(): picked = flattened[jnp.minimum(fill_src, item_count - 1)]]
    all_to_all x1 -> x0, starting transfers between devices: 9.66 us -> none  [local(): lax.all_to_all(outgoing, 'sector', split_axis=0, concat_axis=0, tiled=True)]
  transfers between devices with their start and end apart: 3 -> 0, of which waited for: 3 -> 0; matrix products, arithmetic and copies ran while one was open for 2% -> 0% of each run, Pallas kernels for 0% -> 0%
where the time goes in v1:
time: 53.8 us; the launch traced here: 53.7 us
  Pallas kernels  52.1 us (97%)
  local copies, waits for them, and re-layouts  1.57 us (3%)
    pallas_call x1, Pallas kernels, local(): pl.pallas_call(kernel, out_shape=jax.ShapeDtypeStruct((S, N // J, N), BF)...  52.1 us
    unnamed x1, local copies, waits for them, and re-layouts  1.57 us

profile of v1, /device:TPU:1, one launch (start us, length us, event | category | flops | bytes accessed | tf_op | source)
XLA Modules:
  0.0 53.7 jit_solution(11126275658397410656)
XLA Ops:
  0.0 52.1 %shard_map.64 = bf16[8,32,256]{2,1,0:T(8,128)(2,1)} custom-call(bf16[8,32,256]{2,1,0:T(8,128)(2,1)} %wf.1, bf16[8,8,4,2,2,16,256]{6,5,4,3,2,1,0:T(8,128)(2,1)} %bitcast.1, bf16[8,256,256]{2,1,0:T(8,128)(2,1)} %right.1, s32[8]{0:T(128)} %types.1, s32[2,256]{1,0:T(2,128)} %slots.1, s32[256]{0:T(256)} %rows.1), custom_call_target="tpu_custom_call" | custom-call | tf_op jit(solution)/shard_map/pallas_call | solution.py:232
  52.1 1.6 %copy.8 = bf16[8,32,256]{2,1,0:T(8,128)(2,1)} copy(bf16[8,32,256]{2,1,0:T(8,128)(2,1)} %shard_map.64) | data formatting | bytes 262144

commit v2 on v1

v2 whole, which is shorter than its diff:
```python
import jax
import jax.numpy as jnp
from jax import lax
from jax.experimental import pallas as pl
from jax.experimental.pallas import tpu as pltpu
from jax.sharding import PartitionSpec as P

MESH = pl.DeviceIdType.MESH
BF, F32 = jnp.bfloat16, jnp.float32
N = 256
S = 8
K = 8
G = 2
Y = 4
J = 8
D = 32
H = 2
R = N // J // H
C = 4
SC = S // C
Q = 2
W = N // Q
X, Z = 4, 8
CHUNKS = [(h, q) for h in range(H) for q in range(Q)]
STEPS = sorted(
    ((dx, dz) for dx in range(X) for dz in range(Z) if dx or dz),
    key=lambda step: (-min(step[0], X - step[0]) - min(step[1], Z - step[1]), step[1] % 2, step),
)


def kernel(
    wf, left, right, types_h, slots_h, rows_h,
    out,
    left_v, right_v, rcat, gath, masked, half, own, d2d_out, d2d_in, y_out, y_in,
    items, a2a_out, a2a_in, tab_v, tab, types, slots, rows,
    left_sem, misc_sem, ag_send, ag_recv, d2d_send, d2d_recv, y_send, y_recv, a2a_send, a2a_recv, known,
):
    me_s, me_t = lax.axis_index("sector"), lax.axis_index("term")
    x, z, y, c = me_s // Z, me_s % Z, me_t // 2, me_t % 2
    sib = y * 2 + (1 - c)

    def y_peer(d):
        return lax.rem(y + d, Y) * 2 + c

    def z_peer(d):
        return x * Z + lax.rem(z + d, Z)

    def x_peer(d):
        return lax.rem(x + d, X) * Z + z

    def signal(sem, **to):
        pl.semaphore_signal(sem, inc=1, device_id=to, device_id_type=MESH)

    barrier = pltpu.get_barrier_semaphore()
    signal(barrier, term=sib)
    for d in range(1, Y):
        signal(barrier, term=y_peer(d))
    for d in (1, Z - 1):
        signal(barrier, sector=z_peer(d))
    for d in (1, X - 1):
        signal(barrier, sector=x_peer(d))

    def term_copy(src, dst, send, recv, to):
        return pltpu.make_async_remote_copy(
            src_ref=src, dst_ref=dst, send_sem=send, recv_sem=recv,
            device_id={"term": to}, device_id_type=MESH,
        )

    left_copies = {}

    def load(p):
        for h in range(H):
            for o in range(2):
                side = 1 - c if o == 0 else c
                cp = pltpu.make_async_copy(
                    left.at[:, pl.ds(p * SC, SC), :, side, h], left_v.at[p, h, o], left_sem.at[p, h, o]
                )
                cp.start()
                left_copies[p, h, o] = cp

    own_copy = pltpu.make_async_copy(wf, gath.at[:, me_t], misc_sem.at[1])
    own_copy.start()
    small = []
    for n, (src, dst) in enumerate(((slots_h, slots), (types_h, types), (rows_h, rows))):
        cp = pltpu.make_async_copy(src, dst, misc_sem.at[3 + n])
        cp.start()
        small.append(cp)
    right_copy = pltpu.make_async_copy(right, right_v, misc_sem.at[0])
    right_copy.start()
    load(0)
    own_copy.wait()
    pl.semaphore_wait(barrier, 1 + (Y - 1) + 4)

    pending = []
    first = {}
    for p in range(C):
        mine = gath.at[pl.ds(p * SC, SC), me_t]
        for d in (2, 1, 3):
            cp = term_copy(
                mine, mine, ag_send.at[p, d], ag_recv.at[p, d], y_peer(d)
            )
            cp.start()
            first[p, d] = cp
        cp = term_copy(mine, mine, ag_send.at[p, 0], ag_recv.at[p, 0], sib)
        cp.start()
        first[p, 0] = cp
    for d in (1, Z - 1):
        signal(known.at[0], sector=z_peer(d))
    for d in (1, X - 1):
        signal(known.at[0], sector=x_peer(d))
    for p in range(1, C):
        load(p)

    for cp in small:
        cp.wait()

    lane = lax.broadcasted_iota(jnp.int32, (D, D * S), 1)
    peer = lax.broadcasted_iota(jnp.int32, (D, D * S), 0)
    mine = lax.shift_right_logical(lane, 3) == me_s
    item = jnp.zeros((D, D * S), jnp.int32)
    target = lax.broadcasted_iota(jnp.int32, (S, D * S), 0) + me_s * S
    lane_s = lax.broadcasted_iota(jnp.int32, (S, D * S), 1)
    for g in range(G):
        row = slots[g : g + 1, :]
        hit = mine & (lax.shift_right_logical(row, 3) == peer)
        item = jnp.maximum(item, jnp.where(hit, jnp.bitwise_and(lane, 7) + g * S, 0))
        src = jnp.where(row == target, lax.shift_right_logical(lane_s, 3), 0)
        tab_v[D + g * S : D + (g + 1) * S, :] = jnp.broadcast_to(
            jnp.max(src, axis=1, keepdims=True), (S, 128)
        )
    tab_v[0:D, :] = jnp.broadcast_to(jnp.max(item, axis=1, keepdims=True), (D, 128))
    tab_copy = pltpu.make_async_copy(tab_v, tab, misc_sem.at[2])
    tab_copy.start()

    right_copy.wait()
    for k in range(K):
        for g in range(G):
            value = jnp.where(types[k] == g, right_v[k].astype(F32), 0.0).astype(BF)
            for q in range(Q):
                rcat[q, k * N : (k + 1) * N, g * W : (g + 1) * W] = value[:, q * W : (q + 1) * W]

    def forward(p):
        part = pl.ds(p * SC, SC)
        for d in (1, 3, 2):
            first[p, d].wait_recv()
            owner = lax.rem(y + Y - d, Y) * 2 + c
            block = gath.at[part, owner]
            cp = term_copy(block, block, ag_send.at[p, 3 + d], ag_recv.at[p, 3 + d], sib)
            cp.start()
            first[p, 3 + d] = cp

    def first_product(p):
        first[p, 0].wait_recv()
        for d in (1, 3, 2):
            first[p, 3 + d].wait_recv()
        for h in range(H):
            for o in range(2):
                left_copies[p, h, o].wait()
        row_id = lax.broadcasted_iota(jnp.int32, (N, N), 0)
        for s in range(p * SC, (p + 1) * SC):
            block = gath[s].reshape(N, N).astype(F32)
            masked[s] = jnp.where(row_id < rows[me_s * S + s], block, 0.0).astype(BF)
        for h in range(H):
            for o in range(2):
                for s in range(SC):
                    lhs = left_v[p, h, o, :, s].reshape(K * Y * R, N)
                    res = jnp.dot(lhs, masked[p * SC + s], preferred_element_type=F32).astype(BF)
                    for k in range(K):
                        half[h, o, p * SC + s, :, k * N : (k + 1) * N] = res[k * Y * R : (k + 1) * Y * R]

    def second_product(h, q, o, lo, n):
        lhs = half[h, o, lo : lo + n].reshape(n * Y * R, K * N)
        return jnp.dot(lhs, rcat[q], preferred_element_type=F32).reshape(n, Y, R, G * W)

    def products(i, p, lo, n):
        h, q = CHUNKS[i]
        d2d_out[i, lo : lo + n] = second_product(h, q, 0, lo, n).astype(BF)
        part = pl.ds(lo, n)
        cp = term_copy(d2d_out.at[i, part], d2d_in.at[i, part], d2d_send.at[i, p], d2d_recv.at[i, p], sib)
        cp.start()
        pending.append(cp)
        own[i, lo : lo + n] = second_product(h, q, 1, lo, n)
        return cp

    y_copies = {i: [] for i in range(len(CHUNKS))}

    def send_y(i, p, lo, n, d2d):
        d2d.wait_recv()
        part = pl.ds(lo, n)
        for d in (2, 1, 3):
            to = lax.rem(y + d, Y)
            y_out[i, d - 1, lo : lo + n] = (own[i, part, to] + d2d_in[i, part, to].astype(F32)).astype(BF)
            cp = term_copy(
                y_out.at[i, d - 1, part], y_in.at[i, d - 1, part],
                y_send.at[i, p, d - 1], y_recv.at[i, p, d - 1], y_peer(d),
            )
            cp.start()
            y_copies[i].append(cp)
            pending.append(cp)

    def send_a2a(i):
        for cp in y_copies[i]:
            cp.wait_recv()
        total = own[i, :, y] + d2d_in[i, :, y].astype(F32)
        for d in range(1, Y):
            total = total + y_in[i, d - 1].astype(F32)
        total = total.astype(BF)
        for g in range(G):
            items[i, g * S : (g + 1) * S] = total[:, :, g * W : (g + 1) * W]
        for dx, dz in STEPS:
            p = lax.rem(x + dx, X) * Z + lax.rem(z + dz, Z)
            a2a_out[i, p] = items[i, tab[p, 0]]
            pltpu.make_async_remote_copy(
                src_ref=a2a_out.at[i, p], dst_ref=a2a_in[i].at[me_s],
                send_sem=a2a_send.at[i], recv_sem=a2a_recv.at[i],
                device_id={"sector": p}, device_id_type=MESH,
            ).start()
        a2a_in[i][me_s] = items[i, tab[me_s, 0]]

    def combine(i):
        h, q = CHUNKS[i]
        got = a2a_in[i].at[pl.ds(0, D - 1)]
        pltpu.make_async_copy(got, got, a2a_recv.at[i]).wait()
        row_id = lax.broadcasted_iota(jnp.int32, (R, W), 0) + (me_t * (H * R) + h * R)
        for t in range(S):
            value = a2a_in[i][tab[D + t, 0]].astype(F32) + a2a_in[i][tab[D + S + t, 0]].astype(F32)
            value = jnp.where(row_id < rows[me_s * S + t], value, 0.0)
            out[t, h * R : (h + 1) * R, q * W : (q + 1) * W] = value.astype(BF)

    d2d = {}
    forward(0)
    for p in range(C):
        if p + 1 < C:
            forward(p + 1)
        first_product(p)
        d2d[p] = products(0, p, p * SC, SC)
        if p > 0:
            send_y(0, p - 1, (p - 1) * SC, SC, d2d[p - 1])
        if p == 0:
            pl.semaphore_wait(known.at[0], 4)
            for d in (2, Z - 2):
                signal(known.at[1], sector=z_peer(d))
        if p == 2:
            pl.semaphore_wait(known.at[1], 2)
            for d in range(1, X):
                signal(known.at[2], sector=x_peer(d))
    send_y(0, C - 1, (C - 1) * SC, SC, d2d[C - 1])
    pending += list(first.values())
    for i in range(1, len(CHUNKS)):
        send_y(i, 0, 0, S, products(i, 0, 0, S))
    tab_copy.wait()
    pl.semaphore_wait(known.at[2], X - 1)
    for i in range(len(CHUNKS)):
        send_a2a(i)
    for i in range(len(CHUNKS)):
        combine(i)
    for cp in pending:
        cp.wait_send()
    for i in range(H * Q):
        sent = a2a_out.at[i, pl.ds(0, D - 1)]
        pltpu.make_async_copy(sent, sent, a2a_send.at[i]).wait()


def local(wavefunction, left_ops, right_ops, term_type, target_slots, block_rows):
    left = left_ops.reshape(K, S, Y, 2, H, R, N)
    any_space = pl.BlockSpec(memory_space=pl.ANY)
    vmem = pl.BlockSpec(memory_space=pltpu.VMEM)
    dma = pltpu.SemaphoreType.DMA
    return pl.pallas_call(
        kernel,
        out_shape=pltpu.VMEM((S, N // J, N), BF),
        in_specs=[any_space] * 6,
        out_specs=vmem,
        scratch_shapes=[
            pltpu.VMEM((C, H, 2, K, SC, Y, R, N), BF),
            pltpu.VMEM((K, N, N), BF),
            pltpu.VMEM((Q, K * N, G * W), BF),
            pltpu.VMEM((S, J, N // J, N), BF),
            pltpu.VMEM((S, N, N), BF),
            pltpu.VMEM((H, 2, S, Y * R, K * N), BF),
            pltpu.VMEM((H * Q, S, Y, R, G * W), F32),
            pltpu.VMEM((H * Q, S, Y, R, G * W), BF),
            pltpu.VMEM((H * Q, S, Y, R, G * W), BF),
            pltpu.VMEM((H * Q, Y - 1, S, R, G * W), BF),
            pltpu.VMEM((H * Q, Y - 1, S, R, G * W), BF),
            pltpu.VMEM((H * Q, G * S, R, W), BF),
            pltpu.VMEM((H * Q, D, R, W), BF),
            [pltpu.VMEM((D, R, W), BF)] * (H * Q),
            pltpu.VMEM((D + G * S, 128), jnp.int32),
            pltpu.SMEM((D + G * S, 128), jnp.int32),
            pltpu.SMEM((K,), jnp.int32),
            pltpu.VMEM((G, D * S), jnp.int32),
            pltpu.SMEM((D * S,), jnp.int32),
            dma((C, H, 2)),
            dma((6,)),
            dma((C, 7)),
            dma((C, 7)),
            dma((H * Q, C)),
            dma((H * Q, C)),
            dma((H * Q, C, Y - 1)),
            dma((H * Q, C, Y - 1)),
            dma((H * Q,)),
            dma((H * Q,)),
            pltpu.SemaphoreType.REGULAR((3,)),
        ],
        compiler_params=pltpu.CompilerParams(
            collective_id=0, has_side_effects=True, vmem_limit_bytes=56 * 1024 * 1024
        ),
    )(wavefunction, left, right_ops, term_type, target_slots, block_rows)


def solution(mesh):
    in_specs = (
        P("sector", "term", None),
        P("term", "sector", None, None),
        P("term", None, None),
        P("term"),
        P(),
        P(),
    )
    out_specs = P("sector", "term", None)
    return jax.shard_map(local, mesh=mesh, in_specs=in_specs, out_specs=out_specs, check_vma=False)
```

time: 53.8 us -> 45.8 us (0.85)
  Pallas kernels: 52.1 us -> 45.1 us
  local copies, waits for them, and re-layouts: 1.57 us -> 0.66 us
    pallas_call x1, Pallas kernels: 52.1 us -> 45.1 us  [local(): pl.pallas_call(kernel, out_shape=pltpu.VMEM((S, N // J, N), BF), in_specs...]
    unnamed x1, local copies, waits for them, and re-layouts: 1.57 us -> 0.66 us
where the time goes in v2:
time: 45.8 us; the launch traced here: 45.7 us
  Pallas kernels  45.1 us (98%)
  local copies, waits for them, and re-layouts  0.66 us (1%)
    pallas_call x1, Pallas kernels, local(): pl.pallas_call(kernel, out_shape=pltpu.VMEM((S, N // J, N), BF), in_specs...  45.1 us

profile of v2, /device:TPU:1, one launch (start us, length us, event | category | flops | bytes accessed | tf_op | source)
XLA Modules:
  0.0 45.7 jit_solution(5759407546852347912)
XLA Ops:
  0.0 45.1 %shard_map.64 = bf16[8,32,256]{2,1,0:T(8,128)(2,1)S(1)} custom-call(bf16[8,32,256]{2,1,0:T(8,128)(2,1)} %wf.1, bf16[8,8,4,2,2,16,256]{6,5,4,3,2,1,0:T(8,128)(2,1)} %bitcast.1, bf16[8,256,256]{2,1,0:T(8,128)(2,1)} %right.1, s32[8]{0:T(128)} %types_h.1, s32[2,256]{1,0:T(2,128)} %slots_h.1, s32[256]{0:T(256)} %rows_h.1), custom_call_target="tpu_custom_call" | custom-call | tf_op jit(solution)/shard_map/pallas_call | solution.py:269
  45.1 0.7 %copy.8 = bf16[8,32,256]{2,1,0:T(8,128)(2,1)} copy(bf16[8,32,256]{2,1,0:T(8,128)(2,1)S(1)} %shard_map.64) | data formatting | bytes 262144

commit v3 on v2

--- a/solution.py
+++ b/solution.py
@@ -21,7 +21,7 @@
 Q = 2
 W = N // Q
 X, Z = 4, 8
-CHUNKS = [(h, q) for h in range(H) for q in range(Q)]
+CHUNKS = [(h, q) for q in range(Q) for h in range(H)]
 STEPS = sorted(
     ((dx, dz) for dx in range(X) for dz in range(Z) if dx or dz),
     key=lambda step: (-min(step[0], X - step[0]) - min(step[1], Z - step[1]), step[1] % 2, step),
@@ -168,42 +168,43 @@
                     for k in range(K):
                         half[h, o, p * SC + s, :, k * N : (k + 1) * N] = res[k * Y * R : (k + 1) * Y * R]
 
-    def second_product(h, q, o, lo, n):
-        lhs = half[h, o, lo : lo + n].reshape(n * Y * R, K * N)
-        return jnp.dot(lhs, rcat[q], preferred_element_type=F32).reshape(n, Y, R, G * W)
-
-    def products(i, p, lo, n):
-        h, q = CHUNKS[i]
-        d2d_out[i, lo : lo + n] = second_product(h, q, 0, lo, n).astype(BF)
+    def second_product(q, lhs):
+        shape = lhs.shape[:-2]
+        res = jnp.dot(lhs.reshape(-1, K * N), rcat[q], preferred_element_type=F32)
+        return res.reshape(shape + (Y, R, G * W))
+
+    def send_d2d(q, p, lo, n):
         part = pl.ds(lo, n)
-        cp = term_copy(d2d_out.at[i, part], d2d_in.at[i, part], d2d_send.at[i, p], d2d_recv.at[i, p], sib)
+        cp = term_copy(
+            d2d_out.at[q, :, part], d2d_in.at[q, :, part], d2d_send.at[q, p], d2d_recv.at[q, p], sib
+        )
         cp.start()
         pending.append(cp)
-        own[i, lo : lo + n] = second_product(h, q, 1, lo, n)
         return cp
 
-    y_copies = {i: [] for i in range(len(CHUNKS))}
-
-    def send_y(i, p, lo, n, d2d):
-        d2d.wait_recv()
+    y_copies = {chunk: [] for chunk in CHUNKS}
+
+    def send_y(h, q, p, lo, n):
         part = pl.ds(lo, n)
         for d in (2, 1, 3):
             to = lax.rem(y + d, Y)
-            y_out[i, d - 1, lo : lo + n] = (own[i, part, to] + d2d_in[i, part, to].astype(F32)).astype(BF)
+            value = own[q, h, part, to] + d2d_in[q, h, part, to].astype(F32)
+            y_out[q, h, d - 1, lo : lo + n] = value.astype(BF)
             cp = term_copy(
-                y_out.at[i, d - 1, part], y_in.at[i, d - 1, part],
-                y_send.at[i, p, d - 1], y_recv.at[i, p, d - 1], y_peer(d),
+                y_out.at[q, h, d - 1, part], y_in.at[q, h, d - 1, part],
+                y_send.at[q, h, p, d - 1], y_recv.at[q, h, p, d - 1], y_peer(d),
             )
             cp.start()
-            y_copies[i].append(cp)
+            y_copies[h, q].append(cp)
             pending.append(cp)
 
     def send_a2a(i):
-        for cp in y_copies[i]:
+        h, q = CHUNKS[i]
+        for cp in y_copies[h, q]:
             cp.wait_recv()
-        total = own[i, :, y] + d2d_in[i, :, y].astype(F32)
+        total = own[q, h, :, y] + d2d_in[q, h, :, y].astype(F32)
         for d in range(1, Y):
-            total = total + y_in[i, d - 1].astype(F32)
+            total = total + y_in[q, h, d - 1].astype(F32)
         total = total.astype(BF)
         for g in range(G):
             items[i, g * S : (g + 1) * S] = total[:, :, g * W : (g + 1) * W]
@@ -227,15 +228,20 @@
             value = jnp.where(row_id < rows[me_s * S + t], value, 0.0)
             out[t, h * R : (h + 1) * R, q * W : (q + 1) * W] = value.astype(BF)
 
-    d2d = {}
+    shared = {}
     forward(0)
     for p in range(C):
+        lo = p * SC
         if p + 1 < C:
             forward(p + 1)
         first_product(p)
-        d2d[p] = products(0, p, p * SC, SC)
+        res = second_product(0, half[:, :, lo : lo + SC])
+        d2d_out[0, :, lo : lo + SC] = res[:, 0].astype(BF)
+        shared[p] = send_d2d(0, p, lo, SC)
+        own[0, :, lo : lo + SC] = res[:, 1]
         if p > 0:
-            send_y(0, p - 1, (p - 1) * SC, SC, d2d[p - 1])
+            shared[p - 1].wait_recv()
+            send_y(0, 0, p - 1, lo - SC, SC)
         if p == 0:
             pl.semaphore_wait(known.at[0], 4)
             for d in (2, Z - 2):
@@ -244,10 +250,17 @@
             pl.semaphore_wait(known.at[1], 2)
             for d in range(1, X):
                 signal(known.at[2], sector=x_peer(d))
-    send_y(0, C - 1, (C - 1) * SC, SC, d2d[C - 1])
     pending += list(first.values())
-    for i in range(1, len(CHUNKS)):
-        send_y(i, 0, 0, S, products(i, 0, 0, S))
+    d2d_out[1, 0] = second_product(1, half[0, 0]).astype(BF)
+    shared[C - 1].wait_recv()
+    send_y(0, 0, C - 1, S - SC, SC)
+    send_y(1, 0, 0, 0, S)
+    d2d_out[1, 1] = second_product(1, half[1, 0]).astype(BF)
+    right_half = send_d2d(1, 0, 0, S)
+    own[1] = second_product(1, half[:, 1])
+    right_half.wait_recv()
+    for h in range(H):
+        send_y(h, 1, 0, 0, S)
     tab_copy.wait()
     pl.semaphore_wait(known.at[2], X - 1)
     for i in range(len(CHUNKS)):
@@ -278,11 +291,11 @@
             pltpu.VMEM((S, J, N // J, N), BF),
             pltpu.VMEM((S, N, N), BF),
             pltpu.VMEM((H, 2, S, Y * R, K * N), BF),
-            pltpu.VMEM((H * Q, S, Y, R, G * W), F32),
-            pltpu.VMEM((H * Q, S, Y, R, G * W), BF),
-            pltpu.VMEM((H * Q, S, Y, R, G * W), BF),
-            pltpu.VMEM((H * Q, Y - 1, S, R, G * W), BF),
-            pltpu.VMEM((H * Q, Y - 1, S, R, G * W), BF),
+            pltpu.VMEM((Q, H, S, Y, R, G * W), F32),
+            pltpu.VMEM((Q, H, S, Y, R, G * W), BF),
+            pltpu.VMEM((Q, H, S, Y, R, G * W), BF),
+            pltpu.VMEM((Q, H, Y - 1, S, R, G * W), BF),
+            pltpu.VMEM((Q, H, Y - 1, S, R, G * W), BF),
             pltpu.VMEM((H * Q, G * S, R, W), BF),
             pltpu.VMEM((H * Q, D, R, W), BF),
             [pltpu.VMEM((D, R, W), BF)] * (H * Q),
@@ -295,10 +308,10 @@
             dma((6,)),
             dma((C, 7)),
             dma((C, 7)),
-            dma((H * Q, C)),
-            dma((H * Q, C)),
-            dma((H * Q, C, Y - 1)),
-            dma((H * Q, C, Y - 1)),
+            dma((Q, C)),
+            dma((Q, C)),
+            dma((Q, H, C, Y - 1)),
+            dma((Q, H, C, Y - 1)),
             dma((H * Q,)),
             dma((H * Q,)),
             pltpu.SemaphoreType.REGULAR((3,)),

time: 45.8 us -> 45.7 us (level)
  no operation moved by 1% of the time
where the time goes in v3:
time: 45.7 us
  Pallas kernels  45 us (98%)
  local copies, waits for them, and re-layouts  0.66 us (1%)
    pallas_call x1, Pallas kernels, local(): pl.pallas_call(kernel, out_shape=pltpu.VMEM((S, N // J, N), BF), in_specs...  45 us

profile of v3, /device:TPU:1, one launch (start us, length us, event | category | flops | bytes accessed | tf_op | source)
XLA Modules:
  0.0 45.7 jit_solution(18032394298786966311)
XLA Ops:
  0.0 45.0 %shard_map.64 = bf16[8,32,256]{2,1,0:T(8,128)(2,1)S(1)} custom-call(bf16[8,32,256]{2,1,0:T(8,128)(2,1)} %wf.1, bf16[8,8,4,2,2,16,256]{6,5,4,3,2,1,0:T(8,128)(2,1)} %bitcast.1, bf16[8,256,256]{2,1,0:T(8,128)(2,1)} %right.1, s32[8]{0:T(128)} %types_h.1, s32[2,256]{1,0:T(2,128)} %slots_h.1, s32[256]{0:T(256)} %rows_h.1), custom_call_target="tpu_custom_call" | custom-call | tf_op jit(solution)/shard_map/pallas_call | solution.py:282
  45.0 0.7 %copy.8 = bf16[8,32,256]{2,1,0:T(8,128)(2,1)} copy(bf16[8,32,256]{2,1,0:T(8,128)(2,1)S(1)} %shard_map.64) | data formatting | bytes 262144

commit v4 on v3

--- a/solution.py
+++ b/solution.py
@@ -16,8 +16,8 @@
 D = 32
 H = 2
 R = N // J // H
-C = 4
-SC = S // C
+PARTS = [(0, 2), (2, 2), (4, 2), (6, 1), (7, 1)]
+C = len(PARTS)
 Q = 2
 W = N // Q
 X, Z = 4, 8
@@ -69,11 +69,12 @@
     left_copies = {}
 
     def load(p):
+        slots_of = pl.ds(*PARTS[p])
         for h in range(H):
             for o in range(2):
                 side = 1 - c if o == 0 else c
                 cp = pltpu.make_async_copy(
-                    left.at[:, pl.ds(p * SC, SC), :, side, h], left_v.at[p, h, o], left_sem.at[p, h, o]
+                    left.at[:, slots_of, :, side, h], left_v.at[h, o, :, slots_of], left_sem.at[p, h, o]
                 )
                 cp.start()
                 left_copies[p, h, o] = cp
@@ -94,7 +95,7 @@
     pending = []
     first = {}
     for p in range(C):
-        mine = gath.at[pl.ds(p * SC, SC), me_t]
+        mine = gath.at[pl.ds(*PARTS[p]), me_t]
         for d in (2, 1, 3):
             cp = term_copy(
                 mine, mine, ag_send.at[p, d], ag_recv.at[p, d], y_peer(d)
@@ -140,7 +141,7 @@
                 rcat[q, k * N : (k + 1) * N, g * W : (g + 1) * W] = value[:, q * W : (q + 1) * W]
 
     def forward(p):
-        part = pl.ds(p * SC, SC)
+        part = pl.ds(*PARTS[p])
         for d in (1, 3, 2):
             first[p, d].wait_recv()
             owner = lax.rem(y + Y - d, Y) * 2 + c
@@ -157,27 +158,26 @@
             for o in range(2):
                 left_copies[p, h, o].wait()
         row_id = lax.broadcasted_iota(jnp.int32, (N, N), 0)
-        for s in range(p * SC, (p + 1) * SC):
+        lo, n = PARTS[p]
+        for s in range(lo, lo + n):
             block = gath[s].reshape(N, N).astype(F32)
             masked[s] = jnp.where(row_id < rows[me_s * S + s], block, 0.0).astype(BF)
-        for h in range(H):
-            for o in range(2):
-                for s in range(SC):
-                    lhs = left_v[p, h, o, :, s].reshape(K * Y * R, N)
-                    res = jnp.dot(lhs, masked[p * SC + s], preferred_element_type=F32).astype(BF)
+        for s in range(lo, lo + n):
+            for h in range(H):
+                for o in range(2):
+                    lhs = left_v[h, o, :, s].reshape(K * Y * R, N)
+                    res = jnp.dot(lhs, masked[s], preferred_element_type=F32).astype(BF)
                     for k in range(K):
-                        half[h, o, p * SC + s, :, k * N : (k + 1) * N] = res[k * Y * R : (k + 1) * Y * R]
+                        half[h, o, s, :, k * N : (k + 1) * N] = res[k * Y * R : (k + 1) * Y * R]
 
     def second_product(q, lhs):
         shape = lhs.shape[:-2]
         res = jnp.dot(lhs.reshape(-1, K * N), rcat[q], preferred_element_type=F32)
         return res.reshape(shape + (Y, R, G * W))
 
-    def send_d2d(q, p, lo, n):
-        part = pl.ds(lo, n)
-        cp = term_copy(
-            d2d_out.at[q, :, part], d2d_in.at[q, :, part], d2d_send.at[q, p], d2d_recv.at[q, p], sib
-        )
+    def send_d2d(q, h, nh, p, lo, n):
+        at = (q, pl.ds(h, nh), pl.ds(lo, n))
+        cp = term_copy(d2d_out.at[at], d2d_in.at[at], d2d_send.at[q, h, p], d2d_recv.at[q, h, p], sib)
         cp.start()
         pending.append(cp)
         return cp
@@ -208,14 +208,19 @@
         total = total.astype(BF)
         for g in range(G):
             items[i, g * S : (g + 1) * S] = total[:, :, g * W : (g + 1) * W]
-        for dx, dz in STEPS:
-            p = lax.rem(x + dx, X) * Z + lax.rem(z + dz, Z)
-            a2a_out[i, p] = items[i, tab[p, 0]]
-            pltpu.make_async_remote_copy(
-                src_ref=a2a_out.at[i, p], dst_ref=a2a_in[i].at[me_s],
-                send_sem=a2a_send.at[i], recv_sem=a2a_recv.at[i],
-                device_id={"sector": p}, device_id_type=MESH,
-            ).start()
+        for at in range(0, len(STEPS), 8):
+            peers = [
+                lax.rem(x + dx, X) * Z + lax.rem(z + dz, Z) for dx, dz in STEPS[at : at + 8]
+            ]
+            picked = [items[i, tab[p, 0]] for p in peers]
+            for p, value in zip(peers, picked):
+                a2a_out[i, p] = value
+            for p in peers:
+                pltpu.make_async_remote_copy(
+                    src_ref=a2a_out.at[i, p], dst_ref=a2a_in[i].at[me_s],
+                    send_sem=a2a_send.at[i], recv_sem=a2a_recv.at[i],
+                    device_id={"sector": p}, device_id_type=MESH,
+                ).start()
         a2a_in[i][me_s] = items[i, tab[me_s, 0]]
 
     def combine(i):
@@ -223,25 +228,31 @@
         got = a2a_in[i].at[pl.ds(0, D - 1)]
         pltpu.make_async_copy(got, got, a2a_recv.at[i]).wait()
         row_id = lax.broadcasted_iota(jnp.int32, (R, W), 0) + (me_t * (H * R) + h * R)
+        both = [[a2a_in[i][tab[D + g * S + t, 0]] for g in range(G)] for t in range(S)]
         for t in range(S):
-            value = a2a_in[i][tab[D + t, 0]].astype(F32) + a2a_in[i][tab[D + S + t, 0]].astype(F32)
+            value = both[t][0].astype(F32) + both[t][1].astype(F32)
             value = jnp.where(row_id < rows[me_s * S + t], value, 0.0)
             out[t, h * R : (h + 1) * R, q * W : (q + 1) * W] = value.astype(BF)
 
     shared = {}
+
+    def send_y_part(p):
+        shared[p].wait_recv()
+        for h in range(H):
+            send_y(h, 0, p, *PARTS[p])
+
     forward(0)
     for p in range(C):
-        lo = p * SC
+        lo, n = PARTS[p]
+        first_product(p)
         if p + 1 < C:
             forward(p + 1)
-        first_product(p)
-        res = second_product(0, half[:, :, lo : lo + SC])
-        d2d_out[0, :, lo : lo + SC] = res[:, 0].astype(BF)
-        shared[p] = send_d2d(0, p, lo, SC)
-        own[0, :, lo : lo + SC] = res[:, 1]
+        res = second_product(0, half[:, :, lo : lo + n])
+        d2d_out[0, :, lo : lo + n] = res[:, 0].astype(BF)
+        shared[p] = send_d2d(0, 0, H, p, lo, n)
+        own[0, :, lo : lo + n] = res[:, 1]
         if p > 0:
-            shared[p - 1].wait_recv()
-            send_y(0, 0, p - 1, lo - SC, SC)
+            send_y_part(p - 1)
         if p == 0:
             pl.semaphore_wait(known.at[0], 4)
             for d in (2, Z - 2):
@@ -251,16 +262,18 @@
             for d in range(1, X):
                 signal(known.at[2], sector=x_peer(d))
     pending += list(first.values())
-    d2d_out[1, 0] = second_product(1, half[0, 0]).astype(BF)
-    shared[C - 1].wait_recv()
-    send_y(0, 0, C - 1, S - SC, SC)
-    send_y(1, 0, 0, 0, S)
-    d2d_out[1, 1] = second_product(1, half[1, 0]).astype(BF)
-    right_half = send_d2d(1, 0, 0, S)
-    own[1] = second_product(1, half[:, 1])
-    right_half.wait_recv()
+    right_half = {}
     for h in range(H):
-        send_y(h, 1, 0, 0, S)
+        d2d_out[1, h] = second_product(1, half[h, 0]).astype(BF)
+        right_half[h] = send_d2d(1, h, 1, 0, 0, S)
+        if h == 0:
+            send_y_part(C - 1)
+        else:
+            right_half[0].wait_recv()
+            send_y(0, 1, 0, 0, S)
+        own[1, h] = second_product(1, half[h, 1])
+    right_half[1].wait_recv()
+    send_y(1, 1, 0, 0, S)
     tab_copy.wait()
     pl.semaphore_wait(known.at[2], X - 1)
     for i in range(len(CHUNKS)):
@@ -285,7 +298,7 @@
         in_specs=[any_space] * 6,
         out_specs=vmem,
         scratch_shapes=[
-            pltpu.VMEM((C, H, 2, K, SC, Y, R, N), BF),
+            pltpu.VMEM((H, 2, K, S, Y, R, N), BF),
             pltpu.VMEM((K, N, N), BF),
             pltpu.VMEM((Q, K * N, G * W), BF),
             pltpu.VMEM((S, J, N // J, N), BF),
@@ -308,8 +321,8 @@
             dma((6,)),
             dma((C, 7)),
             dma((C, 7)),
-            dma((Q, C)),
-            dma((Q, C)),
+            dma((Q, H, C)),
+            dma((Q, H, C)),
             dma((Q, H, C, Y - 1)),
             dma((Q, H, C, Y - 1)),
             dma((H * Q,)),

time: 45.7 us -> 45.9 us (level)
  no operation moved by 1% of the time
where the time goes in v4:
time: 45.9 us; the launch traced here: 45.8 us
  Pallas kernels  45.1 us (98%)
  local copies, waits for them, and re-layouts  0.66 us (1%)
    pallas_call x1, Pallas kernels, local(): pl.pallas_call(kernel, out_shape=pltpu.VMEM((S, N // J, N), BF), in_specs...  45.1 us

profile of v4, /device:TPU:1, one launch (start us, length us, event | category | flops | bytes accessed | tf_op | source)
XLA Modules:
  0.0 45.8 jit_solution(1041336133544105713)
XLA Ops:
  0.0 45.1 %shard_map.64 = bf16[8,32,256]{2,1,0:T(8,128)(2,1)S(1)} custom-call(bf16[8,32,256]{2,1,0:T(8,128)(2,1)} %wf.1, bf16[8,8,4,2,2,16,256]{6,5,4,3,2,1,0:T(8,128)(2,1)} %bitcast.1, bf16[8,256,256]{2,1,0:T(8,128)(2,1)} %right.1, s32[8]{0:T(128)} %types_h.1, s32[2,256]{1,0:T(2,128)} %slots_h.1, s32[256]{0:T(256)} %rows_h.1), custom_call_target="tpu_custom_call" | custom-call | tf_op jit(solution)/shard_map/pallas_call | solution.py:295
  45.1 0.7 %copy.8 = bf16[8,32,256]{2,1,0:T(8,128)(2,1)} copy(bf16[8,32,256]{2,1,0:T(8,128)(2,1)S(1)} %shard_map.64) | data formatting | bytes 262144

commit v5 on v4

--- a/solution.py
+++ b/solution.py
@@ -16,7 +16,7 @@
 D = 32
 H = 2
 R = N // J // H
-PARTS = [(0, 2), (2, 2), (4, 2), (6, 1), (7, 1)]
+PARTS = [(0, 3), (3, 3), (6, 2)]
 C = len(PARTS)
 Q = 2
 W = N // Q
@@ -257,7 +257,7 @@
             pl.semaphore_wait(known.at[0], 4)
             for d in (2, Z - 2):
                 signal(known.at[1], sector=z_peer(d))
-        if p == 2:
+        if p == 1:
             pl.semaphore_wait(known.at[1], 2)
             for d in range(1, X):
                 signal(known.at[2], sector=x_peer(d))

time: 45.9 us -> 46.7 us (1.017)
  Pallas kernels: 45.1 us -> 45.9 us
    pallas_call x1, Pallas kernels: 45.1 us -> 45.9 us  [local(): pl.pallas_call(kernel, out_shape=pltpu.VMEM((S, N // J, N), BF), in_specs...]
where the time goes in v5:
time: 46.7 us; the launch traced here: 46.6 us
  Pallas kernels  45.9 us (98%)
  local copies, waits for them, and re-layouts  0.66 us (1%)
    pallas_call x1, Pallas kernels, local(): pl.pallas_call(kernel, out_shape=pltpu.VMEM((S, N // J, N), BF), in_specs...  45.9 us

profile of v5, /device:TPU:1, one launch (start us, length us, event | category | flops | bytes accessed | tf_op | source)
XLA Modules:
  0.0 46.6 jit_solution(8003179242941568704)
XLA Ops:
  0.0 45.9 %shard_map.64 = bf16[8,32,256]{2,1,0:T(8,128)(2,1)S(1)} custom-call(bf16[8,32,256]{2,1,0:T(8,128)(2,1)} %wf.1, bf16[8,8,4,2,2,16,256]{6,5,4,3,2,1,0:T(8,128)(2,1)} %bitcast.1, bf16[8,256,256]{2,1,0:T(8,128)(2,1)} %right.1, s32[8]{0:T(128)} %types_h.1, s32[2,256]{1,0:T(2,128)} %slots_h.1, s32[256]{0:T(256)} %rows_h.1), custom_call_target="tpu_custom_call" | custom-call | tf_op jit(solution)/shard_map/pallas_call | solution.py:295
  45.9 0.7 %copy.8 = bf16[8,32,256]{2,1,0:T(8,128)(2,1)} copy(bf16[8,32,256]{2,1,0:T(8,128)(2,1)S(1)} %shard_map.64) | data formatting | bytes 262144

commit v6 on v5

--- a/solution.py
+++ b/solution.py
@@ -238,8 +238,7 @@
 
     def send_y_part(p):
         shared[p].wait_recv()
-        for h in range(H):
-            send_y(h, 0, p, *PARTS[p])
+        send_y(0, 0, p, *PARTS[p])
 
     forward(0)
     for p in range(C):
@@ -247,10 +246,10 @@
         first_product(p)
         if p + 1 < C:
             forward(p + 1)
-        res = second_product(0, half[:, :, lo : lo + n])
-        d2d_out[0, :, lo : lo + n] = res[:, 0].astype(BF)
-        shared[p] = send_d2d(0, 0, H, p, lo, n)
-        own[0, :, lo : lo + n] = res[:, 1]
+        res = second_product(0, half[0, :, lo : lo + n])
+        d2d_out[0, 0, lo : lo + n] = res[0].astype(BF)
+        shared[p] = send_d2d(0, 0, 1, p, lo, n)
+        own[0, 0, lo : lo + n] = res[1]
         if p > 0:
             send_y_part(p - 1)
         if p == 0:
@@ -262,18 +261,19 @@
             for d in range(1, X):
                 signal(known.at[2], sector=x_peer(d))
     pending += list(first.values())
-    right_half = {}
-    for h in range(H):
-        d2d_out[1, h] = second_product(1, half[h, 0]).astype(BF)
-        right_half[h] = send_d2d(1, h, 1, 0, 0, S)
-        if h == 0:
+    last = None
+    for h, q in CHUNKS[1:]:
+        d2d_out[q, h] = second_product(q, half[h, 0]).astype(BF)
+        whole = send_d2d(q, h, 1, 0, 0, S)
+        if last is None:
             send_y_part(C - 1)
         else:
-            right_half[0].wait_recv()
-            send_y(0, 1, 0, 0, S)
-        own[1, h] = second_product(1, half[h, 1])
-    right_half[1].wait_recv()
-    send_y(1, 1, 0, 0, S)
+            last[2].wait_recv()
+            send_y(last[0], last[1], 0, 0, S)
+        own[q, h] = second_product(q, half[h, 1])
+        last = (h, q, whole)
+    last[2].wait_recv()
+    send_y(last[0], last[1], 0, 0, S)
     tab_copy.wait()
     pl.semaphore_wait(known.at[2], X - 1)
     for i in range(len(CHUNKS)):

time: 46.7 us -> 43.9 us (0.940)
  Pallas kernels: 45.9 us -> 43.1 us
    pallas_call x1, Pallas kernels: 45.9 us -> 43.1 us  [local(): pl.pallas_call(kernel, out_shape=pltpu.VMEM((S, N // J, N), BF), in_specs...]
where the time goes in v6:
time: 43.9 us; the launch traced here: 43.8 us
  Pallas kernels  43.1 us (98%)
  local copies, waits for them, and re-layouts  0.66 us (2%)
    pallas_call x1, Pallas kernels, local(): pl.pallas_call(kernel, out_shape=pltpu.VMEM((S, N // J, N), BF), in_specs...  43.1 us

profile of v6, /device:TPU:1, one launch (start us, length us, event | category | flops | bytes accessed | tf_op | source)
XLA Modules:
  0.0 43.8 jit_solution(5896851138211569415)
XLA Ops:
  0.0 43.1 %shard_map.64 = bf16[8,32,256]{2,1,0:T(8,128)(2,1)S(1)} custom-call(bf16[8,32,256]{2,1,0:T(8,128)(2,1)} %wf.1, bf16[8,8,4,2,2,16,256]{6,5,4,3,2,1,0:T(8,128)(2,1)} %bitcast.1, bf16[8,256,256]{2,1,0:T(8,128)(2,1)} %right.1, s32[8]{0:T(128)} %types_h.1, s32[2,256]{1,0:T(2,128)} %slots_h.1, s32[256]{0:T(256)} %rows_h.1), custom_call_target="tpu_custom_call" | custom-call | tf_op jit(solution)/shard_map/pallas_call | solution.py:295
  43.1 0.7 %copy.8 = bf16[8,32,256]{2,1,0:T(8,128)(2,1)} copy(bf16[8,32,256]{2,1,0:T(8,128)(2,1)S(1)} %shard_map.64) | data formatting | bytes 262144
